TPU v7x, 32 devices: a whole 2x2x4 slice. The times are simulated.
32 devices in a mesh: ctx: 16 (over z, x, core), tp: 2 (over y).
Axes of the slice: x: 2, y: 2, z: 4, core: 2. Of those that a mesh axis runs over, the one named last changes fastest.
Arguments:
- tokens: bfloat16 [2048, 2048], P('ctx'), may hold values from -6 to 6
- block_order: int32 [32], replicated, may hold values from 0 to 31, each once
- ln_gain: float32 [2048], replicated, may hold values from 0.1 to 1.9
- ln_bias: float32 [2048], replicated, may hold values from -1.8 to 1.8
- qkv_weight: bfloat16 [2048, 3, 2048], P('ctx', None, 'tp'), may hold values from -0.125 to 0.125
- qkv_bias: float32 [3, 2048], P(None, 'tp'), may hold values from -3 to 3
- out_weight: bfloat16 [2048, 2048], P('ctx', 'tp'), may hold values from -0.5 to 0.5
- fc1_weight: bfloat16 [2048, 8192], P('ctx', 'tp'), may hold values from -0.125 to 0.125
- fc1_bias: float32 [8192], P('tp'), may hold values from -3 to 3
- fc2_weight: bfloat16 [2048, 8192], P('ctx', 'tp'), may hold values from -0.09375 to 0.09375
- out_bias: float32 [2048], replicated, may hold values from -3 to 3
- cotangent: bfloat16 [2048, 2048], P('ctx'), may hold values from -6 to 6
Outputs:
- output: float32 [2048, 2048], P('ctx')
- input_grad: float32 [2048, 2048], P('ctx')
- ln_gain_grad: float32 [2048], replicated
- ln_bias_grad: float32 [2048], replicated
- qkv_weight_grad: float32 [2048, 3, 2048], P('ctx', None, 'tp')
- qkv_bias_grad: float32 [3, 2048], P(None, 'tp')
- out_weight_grad: float32 [2048, 2048], P('ctx', 'tp')
- fc1_weight_grad: float32 [2048, 8192], P('ctx', 'tp')
- fc1_bias_grad: float32 [8192], P('tp')
- fc2_weight_grad: float32 [2048, 8192], P('ctx', 'tp')
- out_bias_grad: float32 [2048], replicated
Inputs may be any that keep to these rules, and one draw needn't show every extreme that they name: block_order is a permutation: each of the 32 half-blocks of 64 positions is held by exactly one pair of rows.
All inputs are finite; a program needn't handle non-finite values.
Results may differ from a plain program's by a relative error of at most 0.015.
Values may be sent and summed in bfloat16 or wider, within the bound.
A program may use at most 256 MiB of HBM per device.

v0:
```python
import math

import jax
import jax.numpy as jnp
from jax import lax
from jax.sharding import PartitionSpec as P

HEAD = 64
ROT = 32


EPS = 1e-05
NEG = -1e30


def passed_along(value, axis, steps):
    count = lax.axis_size(axis)
    pairs = [(source, (source + steps) % count) for source in range(count)]
    return lax.ppermute(value, axis, pairs)


def tables(positions, width):
    freqs = 10000.0 ** (-(jnp.arange(width // 2, dtype=jnp.float32) * 2.0) / width)
    angles = positions.astype(jnp.float32)[:, None] * freqs[None, :]
    angles = jnp.concatenate([angles, angles], axis=-1)
    return (jnp.cos(angles), jnp.sin(angles))


def rotate(value, cosine, sine):
    width = cosine.shape[-1]
    part = value[..., :width]
    turned = jnp.concatenate([-part[..., width // 2 :], part[..., : width // 2]], axis=-1)
    moved = part * cosine[:, None, :] + turned * sine[:, None, :]
    return jnp.concatenate([moved, value[..., width:]], axis=-1)


def gelu_tanh(value):
    return jax.nn.gelu(value, approximate=True)


def pair_grads(
    query_part,
    dout_part,
    top_part,
    total_part,
    delta_part,
    query_place,
    key_part,
    value_part,
    key_place,
):
    scale = 1.0 / math.sqrt(HEAD)
    visible = (query_place[:, None] >= key_place[None, :])[None]
    scores = (
        jnp.einsum("qhe,khe->hqk", query_part, key_part, preferred_element_type=jnp.float32) * scale
    )
    scores = jnp.where(visible, scores, NEG)
    expo = jnp.where(visible, jnp.exp(scores - top_part[..., None]), 0.0)
    probs = expo / total_part[..., None]
    dprobs = jnp.einsum("qhe,khe->hqk", dout_part, value_part, preferred_element_type=jnp.float32)
    dscore = (probs * (dprobs - delta_part[..., None])).astype(jnp.bfloat16)
    query_grad = (
        jnp.einsum("hqk,khe->qhe", dscore, key_part, preferred_element_type=jnp.float32) * scale
    )
    key_grad = (
        jnp.einsum("hqk,qhe->khe", dscore, query_part, preferred_element_type=jnp.float32) * scale
    )
    dout_scaled = dout_part.astype(jnp.float32) / jnp.transpose(total_part)[..., None]
    value_grad = jnp.einsum(
        "hqk,qhe->khe", expo.astype(jnp.bfloat16), dout_scaled, preferred_element_type=jnp.float32
    )
    return (query_grad, key_grad, value_grad)


def local(
    tokens,
    block_order,
    ln_gain,
    ln_bias,
    qkv_weight,
    qkv_bias,
    out_weight,
    fc1_weight,
    fc1_bias,
    fc2_weight,
    out_bias,
    cotangent,
):
    devices = lax.axis_size("ctx")
    myself = lax.axis_index("ctx")
    rows_here = tokens.shape[0]
    half = rows_here // 2
    local_width = qkv_weight.shape[2]
    heads_here = local_width // HEAD
    scale = 1.0 / math.sqrt(HEAD)
    positions = (block_order[:, None] * half + jnp.arange(half, dtype=jnp.int32)[None, :]).reshape(
        -1
    )

    def place_of(source):
        return lax.dynamic_slice_in_dim(positions, source * rows_here, rows_here)

    own_place = place_of(myself)
    cosine, sine = tables(own_place, ROT)
    inputs = tokens.astype(jnp.float32)
    center = inputs - jnp.mean(inputs, axis=-1, keepdims=True)
    inv_std = lax.rsqrt(jnp.mean(center * center, axis=-1, keepdims=True) + EPS)
    unit = center * inv_std
    normed = (unit * ln_gain + ln_bias).astype(jnp.bfloat16)
    w_qkv, w_out, w_up, w_down = (
        lax.all_gather(qkv_weight, "ctx", axis=0, tiled=True),
        lax.all_gather(out_weight, "ctx", axis=0, tiled=True),
        lax.all_gather(fc1_weight, "ctx", axis=0, tiled=True),
        lax.all_gather(fc2_weight, "ctx", axis=0, tiled=True),
    )
    mixed = jnp.einsum("td,dcf->tcf", normed, w_qkv, preferred_element_type=jnp.float32) + qkv_bias
    queries = rotate(mixed[:, 0].reshape(rows_here, heads_here, HEAD), cosine, sine).astype(
        jnp.bfloat16
    )
    keyset = rotate(mixed[:, 1].reshape(rows_here, heads_here, HEAD), cosine, sine).astype(
        jnp.bfloat16
    )
    valueset = mixed[:, 2].reshape(rows_here, heads_here, HEAD).astype(jnp.bfloat16)
    fold_top = jnp.full((heads_here, rows_here), NEG, jnp.float32)
    key_piece = lax.all_gather(keyset, "ctx", axis=0, tiled=True)
    value_piece = lax.all_gather(valueset, "ctx", axis=0, tiled=True)
    seen = positions
    visible = (own_place[:, None] >= seen[None, :])[None]
    scores = (
        jnp.einsum("qhe,khe->hqk", queries, key_piece, preferred_element_type=jnp.float32) * scale
    )
    scores = jnp.where(visible, scores, NEG)
    newtop = jnp.maximum(fold_top, jnp.max(scores, axis=-1))
    weights = jnp.where(visible, jnp.exp(scores - newtop[..., None]), 0.0)
    fold_total = jnp.sum(weights, axis=-1)
    accum = jnp.einsum(
        "hqk,khe->qhe",
        weights.astype(jnp.bfloat16),
        value_piece,
        preferred_element_type=jnp.float32,
    )
    top, total, accum = (newtop, fold_total, accum)
    attended = accum / jnp.transpose(total)[..., None]
    attended_bf = attended.reshape(rows_here, local_width).astype(jnp.bfloat16)
    attn_part = jnp.einsum("tf,of->to", attended_bf, w_out, preferred_element_type=jnp.float32)
    upward = jnp.dot(normed, w_up, preferred_element_type=jnp.float32) + fc1_bias
    activated, gelu_back = jax.vjp(gelu_tanh, upward)
    activated_bf = activated.astype(jnp.bfloat16)
    mlp_part = jnp.einsum("tf,of->to", activated_bf, w_down, preferred_element_type=jnp.float32)
    branches = lax.psum((attn_part + mlp_part).astype(jnp.bfloat16), "tp").astype(jnp.float32)
    output = inputs + branches + out_bias
    grad_out = cotangent.astype(jnp.float32)
    grad_act = jnp.einsum("to,of->tf", cotangent, w_down, preferred_element_type=jnp.float32)
    grad_up = gelu_back(grad_act)[0].astype(jnp.bfloat16)
    grad_att = jnp.einsum("to,of->tf", cotangent, w_out, preferred_element_type=jnp.float32).astype(
        jnp.bfloat16
    )
    grad_att = grad_att.reshape(rows_here, heads_here, HEAD)
    delta_term = jnp.transpose(jnp.sum(grad_att.astype(jnp.float32) * attended, axis=-1))
    own_q, own_k, own_v = pair_grads(
        queries, grad_att, top, total, delta_term, own_place, keyset, valueset, own_place
    )

    def key_turn(turn, carry):
        key_piece, value_piece, key_grad, value_grad, query_grad = carry
        key_piece, value_piece = passed_along((key_piece, value_piece), "ctx", 1)
        key_grad, value_grad = (
            passed_along(key_grad.astype(jnp.bfloat16), "ctx", 1).astype(key_grad.dtype),
            passed_along(value_grad.astype(jnp.bfloat16), "ctx", 1).astype(value_grad.dtype),
        )
        seen = place_of((myself - turn) % devices)
        part_q, part_k, part_v = pair_grads(
            queries, grad_att, top, total, delta_term, own_place, key_piece, value_piece, seen
        )
        return (key_piece, value_piece, key_grad + part_k, value_grad + part_v, query_grad + part_q)

    ended = lax.fori_loop(1, devices, key_turn, (keyset, valueset, own_k, own_v, own_q))
    key_grad, value_grad = (
        passed_along(ended[2].astype(jnp.bfloat16), "ctx", 1).astype(jnp.float32),
        passed_along(ended[3].astype(jnp.bfloat16), "ctx", 1).astype(jnp.float32),
    )
    query_grad = ended[4]
    back_query = rotate(query_grad, cosine, -sine).astype(jnp.bfloat16)
    back_key = rotate(key_grad, cosine, -sine).astype(jnp.bfloat16)
    back_value = value_grad.astype(jnp.bfloat16)
    grad_mixed = jnp.stack(
        [
            back_query.reshape(rows_here, local_width),
            back_key.reshape(rows_here, local_width),
            back_value.reshape(rows_here, local_width),
        ],
        axis=1,
    )
    grad_normed = jnp.einsum("tcf,dcf->td", grad_mixed, w_qkv, preferred_element_type=jnp.float32)
    grad_normed = grad_normed + jnp.einsum(
        "tf,df->td", grad_up, w_up, preferred_element_type=jnp.float32
    )
    grad_normed = lax.psum(grad_normed.astype(jnp.bfloat16), "tp").astype(jnp.float32)
    grad_unit = grad_normed * ln_gain
    input_grad = grad_out + inv_std * (
        grad_unit
        - jnp.mean(grad_unit, axis=-1, keepdims=True)
        - unit * jnp.mean(grad_unit * unit, axis=-1, keepdims=True)
    )
    small = lax.psum(
        (
            jnp.sum(grad_mixed.astype(jnp.float32), axis=0),
            jnp.sum(grad_up.astype(jnp.float32), axis=0),
            jnp.sum(grad_out, axis=0),
            jnp.sum(unit * grad_normed, axis=0),
            jnp.sum(grad_normed, axis=0),
        ),
        "ctx",
    )
    inner_operand = jnp.concatenate(
        [grad_mixed.reshape(rows_here, 3 * local_width), grad_up], axis=1
    )
    left_part = normed
    inner_rows = lax.psum_scatter(
        jnp.einsum("tr,tc->rc", left_part, inner_operand, preferred_element_type=jnp.float32),
        "ctx",
        scatter_dimension=0,
        tiled=True,
    )
    outer_operand = jnp.concatenate([attended_bf, activated_bf], axis=1)
    left_part = cotangent
    outer_rows = lax.psum_scatter(
        jnp.einsum("tr,tc->rc", left_part, outer_operand, preferred_element_type=jnp.float32),
        "ctx",
        scatter_dimension=0,
        tiled=True,
    )
    qkv_grad = inner_rows[:, : 3 * local_width].reshape(inner_rows.shape[0], 3, local_width)
    fc1_grad = inner_rows[:, 3 * local_width :]
    out_grad = outer_rows[:, :local_width]
    fc2_grad = outer_rows[:, local_width:]
    return (
        output,
        input_grad,
        small[3],
        small[4],
        qkv_grad,
        small[0],
        out_grad,
        fc1_grad,
        small[1],
        fc2_grad,
        small[2],
    )


def solution(mesh):
    placed = (
        P("ctx", None),
        P(),
        P(),
        P(),
        P("ctx", None, "tp"),
        P(None, "tp"),
        P("ctx", "tp"),
        P("ctx", "tp"),
        P("tp"),
        P("ctx", "tp"),
        P(),
        P("ctx", None),
    )
    return jax.shard_map(
        local,
        mesh=mesh,
        in_specs=placed,
        out_specs=(
            P("ctx", None),
            P("ctx", None),
            P(),
            P(),
            P("ctx", None, "tp"),
            P(None, "tp"),
            P("ctx", "tp"),
            P("ctx", "tp"),
            P("tp"),
            P("ctx", "tp"),
            P(),
        ),
        check_vma=False,
    )
```

profile of v0, /device:TPU:0, one launch (start us, length us, event | category | flops | bytes accessed | tf_op | source)
XLA Modules:
  0.0 1793.3 jit_solution(16375981906589065506)
XLA Ops:
  13.4 100.3 %all-gather.7.cloned.1.call-done = bf16[2048,3,1024]{2,0,1:T(8,128)(2,1)} async-done(((bf16[128,3,1024]{2,0,1:T(8,128)(2,1)}), bf16[2048,3,1024]{2,0,1:T(8,128)(2,1)}) %all-gather.7.cloned.1.call-update) | async-done | bytes 12582928 | tf_op jit(solution)/shard_map/all_gather | solution.py:111
  113.7 6.6 convolution_add_fusion.2
  128.2 36.4 %all-gather.13.cloned.1.call-done = bf16[2048,1024]{1,0:T(8,128)(2,1)} async-done(((bf16[128,1024]{1,0:T(8,128)(2,1)}), bf16[2048,1024]{1,0:T(8,128)(2,1)}) %all-gather.13.cloned.1.call-update) | async-done | bytes 4194320 | tf_op jit(solution)/shard_map/all_gather | solution.py:112
  168.4 50.7 %all-gather.11.cloned.1.call-done = bf16[2048,16,64]{0,2,1:T(8,128)(2,1)} async-done(((bf16[128,16,64]{0,2,1:T(8,128)(2,1)}), bf16[2048,16,64]{0,2,1:T(8,128)(2,1)}) %all-gather.11.cloned.1.call-update) | async-done | bytes 4194320 | tf_op jit(solution)/shard_map/all_gather | solution.py:125
  230.3 6.3 fusion.18
  236.6 36.6 %all-gather.9.cloned.1.call-done = bf16[2048,16,64]{0,2,1:T(8,128)(2,1)} async-done(((bf16[128,16,64]{0,2,1:T(8,128)(2,1)}), bf16[2048,16,64]{0,2,1:T(8,128)(2,1)}) %all-gather.9.cloned.1.call-update) | async-done | bytes 4194320 | tf_op jit(solution)/shard_map/all_gather | solution.py:126
  273.1 12.7 fusion.69
  291.0 431.0 %while.23 = (s32[]{:T(128)}, bf16[128,16,64]{0,2,1:T(8,128)(2,1)S(1)}, bf16[128,16,64]{0,2,1:T(8,128)(2,1)S(1)}, bf16[128,16,64]{0,2,1:T(8,128)(2,1)}, bf16[128,...) while((s32[]{:T(128)}, ...), condition=%wide.region_7.8_spmd, body=%wide.region_6.7_spmd.sunk | while | flops 171589648 | bytes 13961728 | solution.py:177
  294.3 10.8 collective-permute-done
  306.4 7.2 collective-permute-done.1
  315.8 6.1 collective-permute-done.2
  323.0 7.5 collective-permute-done.3
  333.9 7.5 collective-permute-done
  342.7 7.1 collective-permute-done.1
  352.1 6.1 collective-permute-done.2
  359.2 7.5 collective-permute-done.3
  370.2 12.5 collective-permute-done
  383.9 7.2 collective-permute-done.1
  393.4 6.1 collective-permute-done.2
  400.5 7.5 collective-permute-done.3
  411.5 12.5 collective-permute-done
  425.3 7.1 collective-permute-done.1
  442.8 7.0 collective-permute-done
  458.2 6.1 collective-permute-done.2
  465.3 7.5 collective-permute-done.3
  476.2 12.6 collective-permute-done
  490.0 7.1 collective-permute-done.1
  507.6 11.8 collective-permute-done
  520.6 7.2 collective-permute-done.1
  530.1 6.1 collective-permute-done.2
  537.2 7.5 collective-permute-done.3
  548.2 12.5 collective-permute-done
  561.9 7.2 collective-permute-done.1
  571.4 6.1 collective-permute-done.2
  578.5 7.5 collective-permute-done.3
  589.5 9.1 collective-permute-done
  685.9 6.9 collective-permute-done
  704.8 6.9 collective-permute-done
  722.4 9.4 fusion.97
  731.9 11.6 convert_reduce_fusion
  743.4 13.1 fusion.96
  756.5 12.8 fusion.98
  776.9 9.9 fusion.24
  786.9 17.9 convolution_bitcast_fusion.1
  807.6 22.2 %fusion.33 = f32[2048,7168]{1,0:T(8,128)} fusion(bf16[128,4096]{1,0:T(8,128)(2,1)} %copy-done.3, bf16[128,3072]{1,0:T(8,128)(2,1)S(1)} %copy.51, bf16[128,2048]{1,0:T(8,128)(2,1)S(1)} %copy-done.1, f32[2048]{0:T(1024)S(1)} %copy-done.8, f32[2048]{0:T(1024)S(1)} %copy-done.7, f32[128]{0:T(128)S(1)} %copy-done.14, f32[128]{0:T(128)S(1)} %copy-done.12), kind=kOutput, calls=%fused_computation.46 | convolution fusion | flops 3763339264 | bytes 61096960 | tf_op jit(solution)/shard_map/tr,tc->rc/dot_general | solution.py:220
  838.5 61.9 %all-reduce = (f32[2048]{0:T(1024)}, f32[2048]{0:T(1024)}, f32[3,1024]{1,0:T(4,128)}, f32[4096]{0:T(1024)}, f32[2048]{0:T(1024)}) all-reduce(f32[2048]{0:T(1024)S(1)} %get-tuple-element.383, f32[2048]{0:T(1024)S(1)} %get-tuple-element.386, f32[3,1024]{1,0:T(4,128)S(1)} %get-tuple-element.424, ...), channel_id=1, replica_groups=mesh['ctx'=16,'tp'=2] {'ctx'}, use_global_device_ids=true, to_apply=%region_12.13 | all-reduce | flops 13312 | bytes 106496 | tf_op jit(solution)/shard_map/psum | solution.py:205
  900.4 338.1 %reduce-scatter.5.cloned.1.call-done = f32[128,5120]{0,1:T(8,128)} async-done(((f32[2048,5120]{0,1:T(8,128)}), f32[128,5120]{0,1:T(8,128)}) %reduce-scatter.5.cloned.1.call-update) | async-done | bytes 2621456 | tf_op jit(solution)/shard_map/reduce_scatter | solution.py:227
  1242.6 537.4 %reduce-scatter.3.cloned.1.call-done = f32[128,7168]{1,0:T(8,128)} async-done(((f32[2048,7168]{1,0:T(8,128)}), f32[128,7168]{1,0:T(8,128)}) %reduce-scatter.3.cloned.1.call-update) | async-done | bytes 3670032 | tf_op jit(solution)/shard_map/reduce_scatter | solution.py:219
  (350 shorter events, 252.0 us)
Async XLA Ops:
  7.2 106.5 %all-gather.7.cloned.1.call-start = ((), (), s32[]{:S(2)}) async-start(), calls=%async_computation.2 | async-start | bytes 13369344 | tf_op jit(solution)/shard_map/all_gather | solution.py:111
  7.9 156.7 %all-gather.13.cloned.1.call-start = ((), (), s32[]{:S(2)}) async-start(), calls=%async_computation.5 | async-start | bytes 4456448 | tf_op jit(solution)/shard_map/all_gather | solution.py:112
  8.7 210.5 %all-gather.11.cloned.1.call-start = ((), (), s32[]{:S(2)}) async-start(), calls=%async_computation.4 | async-start | bytes 4456448 | tf_op jit(solution)/shard_map/all_gather | solution.py:125
  124.4 148.8 %all-gather.9.cloned.1.call-start = ((), (), s32[]{:S(2)}) async-start(), calls=%async_computation.3 | async-start | bytes 4456448 | tf_op jit(solution)/shard_map/all_gather | solution.py:126
  125.3 597.1 %all-gather.17.cloned.1.call-start = ((), (), s32[]{:S(2)}) async-start(), calls=%async_computation.7 | async-start | bytes 17825792 | tf_op jit(solution)/shard_map/all_gather | solution.py:114
  125.9 605.9 %all-gather.15.cloned.1.call-start = ((), (), s32[]{:S(2)}) async-start(), calls=%async_computation.6 | async-start | bytes 17825792 | tf_op jit(solution)/shard_map/all_gather | solution.py:113
  126.5 707.3 %all-reduce.4.cloned.1.call-start = ((), (), s32[]{:S(2)}) async-start(), calls=%async_computation.10 | async-start | bytes 2097152 | tf_op jit(solution)/shard_map/psum | solution.py:150
  291.3 22.2 %collective-permute-start.1 = (bf16[128,16,64]{0,2,1:T(8,128)(2,1)S(1)}, bf16[128,16,64]{0,2,1:T(8,128)(2,1)S(1)}, u32[]{:S(2)}, u32[]{:S(2)}) collective-permute-start(bf16[128,16,64]{0,2,1:T(8,128)(2,1)S(1)} %get-tuple-element.561), channel_id=1, source_target_pairs={{0,2},{2,4},{4,6},{6,8},{8,10},{10,12},{12,14},{14,16},{16,18},{18... | collective-permute-start | bytes 786440 | tf_op jit(solution)/shard_map/while/body/eval_jaxpr/ppermute | solution.py:19
  292.6 29.4 %collective-permute-start.2 = (bf16[128,16,64]{0,2,1:T(8,128)(2,1)}, bf16[128,16,64]{0,2,1:T(8,128)(2,1)S(1)}, u32[]{:S(2)}, u32[]{:S(2)}) collective-permute-start(bf16[128,16,64]{0,2,1:T(8,128)(2,1)} %get-tuple-element.562), channel_id=1, source_target_pairs={{0,2},{2,4},{4,6},{6,8},{8,10},{10,12},{12,14},{14,16},{16,18},{18... | collective-permute-start | bytes 786440 | tf_op jit(solution)/shard_map/while/body/eval_jaxpr/ppermute | solution.py:19
  292.8 37.6 %collective-permute-start.3 = (bf16[128,16,64]{0,2,1:T(8,128)(2,1)}, bf16[128,16,64]{0,2,1:T(8,128)(2,1)S(1)}, u32[]{:S(2)}, u32[]{:S(2)}) collective-permute-start(bf16[128,16,64]{0,2,1:T(8,128)(2,1)} %get-tuple-element.563), channel_id=1, source_target_pairs={{0,2},{2,4},{4,6},{6,8},{8,10},{10,12},{12,14},{14,16},{16,18},{18... | collective-permute-start | bytes 786440 | tf_op jit(solution)/shard_map/while/body/eval_jaxpr/ppermute | solution.py:19
  332.3 17.5 collective-permute-start.1
  332.4 25.9 %collective-permute-start.2 = (bf16[128,16,64]{0,2,1:T(8,128)(2,1)}, bf16[128,16,64]{0,2,1:T(8,128)(2,1)S(1)}, u32[]{:S(2)}, u32[]{:S(2)}) collective-permute-start(bf16[128,16,64]{0,2,1:T(8,128)(2,1)} %get-tuple-element.562), channel_id=1, source_target_pairs={{0,2},{2,4},{4,6},{6,8},{8,10},{10,12},{12,14},{14,16},{16,18},{18... | collective-permute-start | bytes 786440 | tf_op jit(solution)/shard_map/while/body/eval_jaxpr/ppermute | solution.py:19
  332.4 34.3 %collective-permute-start.3 = (bf16[128,16,64]{0,2,1:T(8,128)(2,1)}, bf16[128,16,64]{0,2,1:T(8,128)(2,1)S(1)}, u32[]{:S(2)}, u32[]{:S(2)}) collective-permute-start(bf16[128,16,64]{0,2,1:T(8,128)(2,1)} %get-tuple-element.563), channel_id=1, source_target_pairs={{0,2},{2,4},{4,6},{6,8},{8,10},{10,12},{12,14},{14,16},{16,18},{18... | collective-permute-start | bytes 786440 | tf_op jit(solution)/shard_map/while/body/eval_jaxpr/ppermute | solution.py:19
  368.6 22.5 %collective-permute-start.1 = (bf16[128,16,64]{0,2,1:T(8,128)(2,1)S(1)}, bf16[128,16,64]{0,2,1:T(8,128)(2,1)S(1)}, u32[]{:S(2)}, u32[]{:S(2)}) collective-permute-start(bf16[128,16,64]{0,2,1:T(8,128)(2,1)S(1)} %get-tuple-element.561), channel_id=1, source_target_pairs={{0,2},{2,4},{4,6},{6,8},{8,10},{10,12},{12,14},{14,16},{16,18},{18... | collective-permute-start | bytes 786440 | tf_op jit(solution)/shard_map/while/body/eval_jaxpr/ppermute | solution.py:19
  368.6 30.9 %collective-permute-start.2 = (bf16[128,16,64]{0,2,1:T(8,128)(2,1)}, bf16[128,16,64]{0,2,1:T(8,128)(2,1)S(1)}, u32[]{:S(2)}, u32[]{:S(2)}) collective-permute-start(bf16[128,16,64]{0,2,1:T(8,128)(2,1)} %get-tuple-element.562), channel_id=1, source_target_pairs={{0,2},{2,4},{4,6},{6,8},{8,10},{10,12},{12,14},{14,16},{16,18},{18... | collective-permute-start | bytes 786440 | tf_op jit(solution)/shard_map/while/body/eval_jaxpr/ppermute | solution.py:19
  368.6 39.3 %collective-permute-start.3 = (bf16[128,16,64]{0,2,1:T(8,128)(2,1)}, bf16[128,16,64]{0,2,1:T(8,128)(2,1)S(1)}, u32[]{:S(2)}, u32[]{:S(2)}) collective-permute-start(bf16[128,16,64]{0,2,1:T(8,128)(2,1)} %get-tuple-element.563), channel_id=1, source_target_pairs={{0,2},{2,4},{4,6},{6,8},{8,10},{10,12},{12,14},{14,16},{16,18},{18... | collective-permute-start | bytes 786440 | tf_op jit(solution)/shard_map/while/body/eval_jaxpr/ppermute | solution.py:19
  409.9 14.1 collective-permute-start
  409.9 22.5 %collective-permute-start.1 = (bf16[128,16,64]{0,2,1:T(8,128)(2,1)S(1)}, bf16[128,16,64]{0,2,1:T(8,128)(2,1)S(1)}, u32[]{:S(2)}, u32[]{:S(2)}) collective-permute-start(bf16[128,16,64]{0,2,1:T(8,128)(2,1)S(1)} %get-tuple-element.561), channel_id=1, source_target_pairs={{0,2},{2,4},{4,6},{6,8},{8,10},{10,12},{12,14},{14,16},{16,18},{18... | collective-permute-start | bytes 786440 | tf_op jit(solution)/shard_map/while/body/eval_jaxpr/ppermute | solution.py:19
  409.9 26.6 %collective-permute-start.2 = (bf16[128,16,64]{0,2,1:T(8,128)(2,1)}, bf16[128,16,64]{0,2,1:T(8,128)(2,1)S(1)}, u32[]{:S(2)}, u32[]{:S(2)}) collective-permute-start(bf16[128,16,64]{0,2,1:T(8,128)(2,1)} %get-tuple-element.562), channel_id=1, source_target_pairs={{0,2},{2,4},{4,6},{6,8},{8,10},{10,12},{12,14},{14,16},{16,18},{18... | collective-permute-start | bytes 786440 | tf_op jit(solution)/shard_map/while/body/eval_jaxpr/ppermute | solution.py:19
  409.9 29.4 %collective-permute-start.3 = (bf16[128,16,64]{0,2,1:T(8,128)(2,1)}, bf16[128,16,64]{0,2,1:T(8,128)(2,1)S(1)}, u32[]{:S(2)}, u32[]{:S(2)}) collective-permute-start(bf16[128,16,64]{0,2,1:T(8,128)(2,1)} %get-tuple-element.563), channel_id=1, source_target_pairs={{0,2},{2,4},{4,6},{6,8},{8,10},{10,12},{12,14},{14,16},{16,18},{18... | collective-permute-start | bytes 786440 | tf_op jit(solution)/shard_map/while/body/eval_jaxpr/ppermute | solution.py:19
  441.3 14.6 collective-permute-start.1
  441.3 23.0 %collective-permute-start.2 = (bf16[128,16,64]{0,2,1:T(8,128)(2,1)}, bf16[128,16,64]{0,2,1:T(8,128)(2,1)S(1)}, u32[]{:S(2)}, u32[]{:S(2)}) collective-permute-start(bf16[128,16,64]{0,2,1:T(8,128)(2,1)} %get-tuple-element.562), channel_id=1, source_target_pairs={{0,2},{2,4},{4,6},{6,8},{8,10},{10,12},{12,14},{14,16},{16,18},{18... | collective-permute-start | bytes 786440 | tf_op jit(solution)/shard_map/while/body/eval_jaxpr/ppermute | solution.py:19
  441.3 31.5 %collective-permute-start.3 = (bf16[128,16,64]{0,2,1:T(8,128)(2,1)}, bf16[128,16,64]{0,2,1:T(8,128)(2,1)S(1)}, u32[]{:S(2)}, u32[]{:S(2)}) collective-permute-start(bf16[128,16,64]{0,2,1:T(8,128)(2,1)} %get-tuple-element.563), channel_id=1, source_target_pairs={{0,2},{2,4},{4,6},{6,8},{8,10},{10,12},{12,14},{14,16},{16,18},{18... | collective-permute-start | bytes 786440 | tf_op jit(solution)/shard_map/while/body/eval_jaxpr/ppermute | solution.py:19
  474.7 14.1 collective-permute-start
  474.7 22.5 %collective-permute-start.1 = (bf16[128,16,64]{0,2,1:T(8,128)(2,1)S(1)}, bf16[128,16,64]{0,2,1:T(8,128)(2,1)S(1)}, u32[]{:S(2)}, u32[]{:S(2)}) collective-permute-start(bf16[128,16,64]{0,2,1:T(8,128)(2,1)S(1)} %get-tuple-element.561), channel_id=1, source_target_pairs={{0,2},{2,4},{4,6},{6,8},{8,10},{10,12},{12,14},{14,16},{16,18},{18... | collective-permute-start | bytes 786440 | tf_op jit(solution)/shard_map/while/body/eval_jaxpr/ppermute | solution.py:19
  474.7 25.8 %collective-permute-start.2 = (bf16[128,16,64]{0,2,1:T(8,128)(2,1)}, bf16[128,16,64]{0,2,1:T(8,128)(2,1)S(1)}, u32[]{:S(2)}, u32[]{:S(2)}) collective-permute-start(bf16[128,16,64]{0,2,1:T(8,128)(2,1)} %get-tuple-element.562), channel_id=1, source_target_pairs={{0,2},{2,4},{4,6},{6,8},{8,10},{10,12},{12,14},{14,16},{16,18},{18... | collective-permute-start | bytes 786440 | tf_op jit(solution)/shard_map/while/body/eval_jaxpr/ppermute | solution.py:19
  474.7 28.6 %collective-permute-start.3 = (bf16[128,16,64]{0,2,1:T(8,128)(2,1)}, bf16[128,16,64]{0,2,1:T(8,128)(2,1)S(1)}, u32[]{:S(2)}, u32[]{:S(2)}) collective-permute-start(bf16[128,16,64]{0,2,1:T(8,128)(2,1)} %get-tuple-element.563), channel_id=1, source_target_pairs={{0,2},{2,4},{4,6},{6,8},{8,10},{10,12},{12,14},{14,16},{16,18},{18... | collective-permute-start | bytes 786440 | tf_op jit(solution)/shard_map/while/body/eval_jaxpr/ppermute | solution.py:19
  505.3 14.1 collective-permute-start
  505.3 22.6 %collective-permute-start.1 = (bf16[128,16,64]{0,2,1:T(8,128)(2,1)S(1)}, bf16[128,16,64]{0,2,1:T(8,128)(2,1)S(1)}, u32[]{:S(2)}, u32[]{:S(2)}) collective-permute-start(bf16[128,16,64]{0,2,1:T(8,128)(2,1)S(1)} %get-tuple-element.561), channel_id=1, source_target_pairs={{0,2},{2,4},{4,6},{6,8},{8,10},{10,12},{12,14},{14,16},{16,18},{18... | collective-permute-start | bytes 786440 | tf_op jit(solution)/shard_map/while/body/eval_jaxpr/ppermute | solution.py:19
  505.3 31.0 %collective-permute-start.2 = (bf16[128,16,64]{0,2,1:T(8,128)(2,1)}, bf16[128,16,64]{0,2,1:T(8,128)(2,1)S(1)}, u32[]{:S(2)}, u32[]{:S(2)}) collective-permute-start(bf16[128,16,64]{0,2,1:T(8,128)(2,1)} %get-tuple-element.562), channel_id=1, source_target_pairs={{0,2},{2,4},{4,6},{6,8},{8,10},{10,12},{12,14},{14,16},{16,18},{18... | collective-permute-start | bytes 786440 | tf_op jit(solution)/shard_map/while/body/eval_jaxpr/ppermute | solution.py:19
  505.3 39.4 %collective-permute-start.3 = (bf16[128,16,64]{0,2,1:T(8,128)(2,1)}, bf16[128,16,64]{0,2,1:T(8,128)(2,1)S(1)}, u32[]{:S(2)}, u32[]{:S(2)}) collective-permute-start(bf16[128,16,64]{0,2,1:T(8,128)(2,1)} %get-tuple-element.563), channel_id=1, source_target_pairs={{0,2},{2,4},{4,6},{6,8},{8,10},{10,12},{12,14},{14,16},{16,18},{18... | collective-permute-start | bytes 786440 | tf_op jit(solution)/shard_map/while/body/eval_jaxpr/ppermute | solution.py:19
  546.6 22.5 %collective-permute-start.1 = (bf16[128,16,64]{0,2,1:T(8,128)(2,1)S(1)}, bf16[128,16,64]{0,2,1:T(8,128)(2,1)S(1)}, u32[]{:S(2)}, u32[]{:S(2)}) collective-permute-start(bf16[128,16,64]{0,2,1:T(8,128)(2,1)S(1)} %get-tuple-element.561), channel_id=1, source_target_pairs={{0,2},{2,4},{4,6},{6,8},{8,10},{10,12},{12,14},{14,16},{16,18},{18... | collective-permute-start | bytes 786440 | tf_op jit(solution)/shard_map/while/body/eval_jaxpr/ppermute | solution.py:19
  546.6 30.9 %collective-permute-start.2 = (bf16[128,16,64]{0,2,1:T(8,128)(2,1)}, bf16[128,16,64]{0,2,1:T(8,128)(2,1)S(1)}, u32[]{:S(2)}, u32[]{:S(2)}) collective-permute-start(bf16[128,16,64]{0,2,1:T(8,128)(2,1)} %get-tuple-element.562), channel_id=1, source_target_pairs={{0,2},{2,4},{4,6},{6,8},{8,10},{10,12},{12,14},{14,16},{16,18},{18... | collective-permute-start | bytes 786440 | tf_op jit(solution)/shard_map/while/body/eval_jaxpr/ppermute | solution.py:19
  546.6 39.3 %collective-permute-start.3 = (bf16[128,16,64]{0,2,1:T(8,128)(2,1)}, bf16[128,16,64]{0,2,1:T(8,128)(2,1)S(1)}, u32[]{:S(2)}, u32[]{:S(2)}) collective-permute-start(bf16[128,16,64]{0,2,1:T(8,128)(2,1)} %get-tuple-element.563), channel_id=1, source_target_pairs={{0,2},{2,4},{4,6},{6,8},{8,10},{10,12},{12,14},{14,16},{16,18},{18... | collective-permute-start | bytes 786440 | tf_op jit(solution)/shard_map/while/body/eval_jaxpr/ppermute | solution.py:19
  587.9 16.3 collective-permute-start.2
  587.9 19.1 %collective-permute-start.3 = (bf16[128,16,64]{0,2,1:T(8,128)(2,1)}, bf16[128,16,64]{0,2,1:T(8,128)(2,1)S(1)}, u32[]{:S(2)}, u32[]{:S(2)}) collective-permute-start(bf16[128,16,64]{0,2,1:T(8,128)(2,1)} %get-tuple-element.563), channel_id=1, source_target_pairs={{0,2},{2,4},{4,6},{6,8},{8,10},{10,12},{12,14},{14,16},{16,18},{18... | collective-permute-start | bytes 786440 | tf_op jit(solution)/shard_map/while/body/eval_jaxpr/ppermute | solution.py:19
  608.9 14.1 collective-permute-start.2
  629.8 14.9 collective-permute-start.3
  646.6 14.1 collective-permute-start.2
  646.9 16.7 collective-permute-start.3
  665.5 14.1 collective-permute-start.2
  665.5 16.9 collective-permute-start.3
  684.4 16.9 collective-permute-start.3
  703.2 16.9 collective-permute-start.3
  722.1 52.3 %collective-permute-start.5 = (bf16[128,16,64]{0,2,1:T(8,128)(2,1)}, bf16[128,16,64]{0,2,1:T(8,128)(2,1)S(1)}, u32[]{:S(2)}, u32[]{:S(2)}) collective-permute-start(bf16[128,16,64]{0,2,1:T(8,128)(2,1)} %get-tuple-element.346), channel_id=1, source_target_pairs={{0,2},{2,4},{4,6},{6,8},{8,10},{10,12},{12,14},{14,16},{16,18},{18... | collective-permute-start | bytes 786440 | tf_op jit(solution)/shard_map/ppermute | solution.py:19
  722.1 53.1 %collective-permute-start.4 = (bf16[128,16,64]{0,2,1:T(8,128)(2,1)}, bf16[128,16,64]{0,2,1:T(8,128)(2,1)S(1)}, u32[]{:S(2)}, u32[]{:S(2)}) collective-permute-start(bf16[128,16,64]{0,2,1:T(8,128)(2,1)} %get-tuple-element.345), channel_id=1, source_target_pairs={{0,2},{2,4},{4,6},{6,8},{8,10},{10,12},{12,14},{14,16},{16,18},{18... | collective-permute-start | bytes 786440 | tf_op jit(solution)/shard_map/ppermute | solution.py:19
  786.8 451.7 %reduce-scatter.5.cloned.1.call-start = ((), (), s32[]{:S(2)}) async-start(), calls=%async_computation.9 | async-start | bytes 44564480 | tf_op jit(solution)/shard_map/reduce_scatter | solution.py:227
  804.8 975.2 %reduce-scatter.3.cloned.1.call-start = ((), (), s32[]{:S(2)}) async-start(), calls=%async_computation.8 | async-start | bytes 62390272 | tf_op jit(solution)/shard_map/reduce_scatter | solution.py:219
  (43 other events, 644.0 us)
Sparse Core Ops, SparseCore 0:
  10.2 103.4 all-gather.6
  115.9 48.7 all-gather.12
  167.4 51.7 all-gather.10
  221.7 51.3 all-gather.8
  275.1 152.0 all-gather.16
  429.2 162.1 all-gather.14
  786.9 46.7 all-reduce.3
  838.6 399.8 reduce-scatter.4
  1243.3 536.5 reduce-scatter.2
where the time goes:
time: 1800 us; the launch traced here: 1790 us
  waiting for transfers between devices  1400 us (78%)
  matrix products  232 us (13%)
  blocking collectives  61.9 us (3%)
  local copies, waits for them, and re-layouts  33.6 us (2%)
  other arithmetic  31.4 us (2%)
  starting transfers between devices  21.8 us (1%)
    reduce_scatter x1, waiting for transfers between devices, local(): lax.psum_scatter(jnp.einsum('tr,tc->rc', left_part, inner_operand, prefer...  537 us
    reduce_scatter x1, waiting for transfers between devices, local(): lax.psum_scatter(jnp.einsum('tr,tc->rc', left_part, outer_operand, prefer...  338 us
    ppermute x62, waiting for transfers between devices, passed_along(): return lax.ppermute(value, axis, pairs)  291 us
    all_gather x1, waiting for transfers between devices, local(): lax.all_gather(qkv_weight, 'ctx', axis=0, tiled=True)  100 us
    psum x1, blocking collectives, local(): lax.psum((jnp.sum(grad_mixed.astype(jnp.float32), axis=0), jnp.sum(grad_u...  61.9 us
    all_gather x1, waiting for transfers between devices, local(): key_piece = lax.all_gather(keyset, 'ctx', axis=0, tiled=True)  50.7 us
    all_gather x1, waiting for transfers between devices, local(): value_piece = lax.all_gather(valueset, 'ctx', axis=0, tiled=True)  36.6 us
    all_gather x1, waiting for transfers between devices, local(): lax.all_gather(out_weight, 'ctx', axis=0, tiled=True)  36.4 us
  transfers between devices with their start and end apart: 71, of which 66 were waited for; matrix products, arithmetic and copies ran while one was open for 15% of the time, Pallas kernels for 0%

commit v1 on v0

v1 whole, which is shorter than its diff:
```python
import functools
import math

import jax
import jax.numpy as jnp
from jax import lax
from jax.experimental import pallas as pl
from jax.experimental.pallas import tpu as pltpu
from jax.sharding import PartitionSpec as P

HEAD = 64
ROT = 32
EPS = 1e-05
NEG = -1e30
BF = jnp.bfloat16
F32 = jnp.float32
NN = (((1,), (0,)), ((), ()))
NT = (((1,), (1,)), ((), ()))
TN = (((0,), (0,)), ((), ()))


def mm(left, right, dims=NN):
    return lax.dot_general(left, right, dims, preferred_element_type=F32)


def tables(positions, width):
    freqs = 10000.0 ** (-(jnp.arange(width // 2, dtype=F32) * 2.0) / width)
    angles = positions.astype(F32)[:, None] * freqs[None, :]
    return (jnp.cos(angles), jnp.sin(angles))


def turned(value, cosine, sine):
    half = cosine.shape[-1]
    first, second = value[..., :half], value[..., half : 2 * half]
    return jnp.concatenate(
        [first * cosine - second * sine, second * cosine + first * sine, value[..., 2 * half :]],
        axis=-1,
    )


def attention_kernel(
    block, order_ref, mixed_ref, gatt_ref, cos_ref, sin_ref, att_ref, gmix_ref,
    placed, gplaced, q_s, k_s, v_s, kt_s, vt_s, ga_s, gat_s, st, dk_s, dv_s, att_s, gm_s,
):
    count, width = gatt_ref.shape
    heads = width // HEAD
    halves = order_ref.shape[0]
    half = count // halves
    blocks = count // block
    scale = 1.0 / math.sqrt(HEAD)

    def place(at, carry):
        source = pl.ds(pl.multiple_of(at * half, half), half)
        target = pl.ds(pl.multiple_of(order_ref[at] * half, half), half)
        placed[target, :] = mixed_ref[source, :]
        gplaced[target, :] = gatt_ref[source, :].astype(F32)
        return carry

    lax.fori_loop(0, halves, place, 0)
    below = lax.broadcasted_iota(jnp.int32, (block, block), 0) <= lax.broadcasted_iota(
        jnp.int32, (block, block), 1
    )

    def rows_of(at):
        return pl.ds(pl.multiple_of(at * block, block), block)

    for head in range(heads):
        def column(kind, head=head):
            return pl.ds(kind * width + head * HEAD, HEAD)

        def prepare(at, carry):
            rows = rows_of(at)
            cosine, sine = cos_ref[rows, :], sin_ref[rows, :]
            query = turned(placed[rows, column(0)], cosine, sine).astype(BF)
            key = turned(placed[rows, column(1)], cosine, sine)
            value = placed[rows, column(2)]
            grad = gplaced[rows, pl.ds(head * HEAD, HEAD)]
            q_s[rows, :] = query * jnp.asarray(scale, BF)
            k_s[rows, :] = key.astype(BF)
            v_s[rows, :] = value.astype(BF)
            ga_s[rows, :] = grad.astype(BF)
            keyvalue = jnp.concatenate([key, value], axis=1).T
            kt_s[:, rows] = keyvalue[:HEAD].astype(BF)
            vt_s[:, rows] = keyvalue[HEAD:].astype(BF)
            gat_s[:, rows] = jnp.concatenate([grad, grad], axis=1).T[:HEAD]
            dk_s[rows, :] = jnp.zeros((block, HEAD), F32)
            dv_s[rows, :] = jnp.zeros((block, HEAD), F32)
            return carry

        lax.fori_loop(0, blocks, prepare, 0)

        def query_block(at, carry):
            rows = rows_of(at)
            query, grad = q_s[rows, :], ga_s[rows, :]

            def folded(value):
                return value.reshape(block // 8, 8, block)

            def scored(place, top):
                scores = mm(k_s[rows_of(place), :], query, NT)
                st[rows_of(place), :] = scores
                return jnp.maximum(top, jnp.max(folded(scores), axis=0))

            top = lax.fori_loop(0, at, scored, jnp.full((8, block), NEG, F32))
            scores = jnp.where(below, mm(k_s[rows, :], query, NT), NEG)
            st[rows, :] = scores
            top = jnp.maximum(top, jnp.max(folded(scores), axis=0))
            top = jnp.max(top, axis=0, keepdims=True)

            def weighed(place, state):
                total, summed = state
                expo = jnp.exp(st[rows_of(place), :] - top)
                st[rows_of(place), :] = expo
                total = total + jnp.sum(folded(expo), axis=0)
                return (total, summed + mm(vt_s[:, rows_of(place)], expo.astype(BF)))

            total, summed = lax.fori_loop(
                0, at + 1, weighed, (jnp.zeros((8, block), F32), jnp.zeros((HEAD, block), F32))
            )
            inverse = 1.0 / jnp.sum(total, axis=0, keepdims=True)
            attended = summed * inverse
            delta = jnp.sum(gat_s[:, rows] * attended, axis=0, keepdims=True)

            def back(place, query_grad):
                here = rows_of(place)
                prob = st[here, :] * inverse
                dprob = mm(v_s[here, :], grad, NT)
                dscore = (prob * (dprob - delta)).astype(BF)
                dk_s[here, :] += mm(dscore, query)
                dv_s[here, :] += mm(prob.astype(BF), grad)
                return query_grad + mm(kt_s[:, here], dscore)

            query_grad = lax.fori_loop(0, at + 1, back, jnp.zeros((HEAD, block), F32))
            both = jnp.concatenate([attended, query_grad], axis=0).T
            att_s[rows, pl.ds(head * HEAD, HEAD)] = both[:, :HEAD].astype(BF)
            gm_s[rows, column(0)] = turned(
                both[:, HEAD:] * scale, cos_ref[rows, :], -sin_ref[rows, :]
            ).astype(BF)
            return carry

        lax.fori_loop(0, blocks, query_block, 0)

        def finish(at, carry):
            rows = rows_of(at)
            gm_s[rows, column(1)] = turned(dk_s[rows, :], cos_ref[rows, :], -sin_ref[rows, :]).astype(BF)
            gm_s[rows, column(2)] = dv_s[rows, :].astype(BF)
            return carry

        lax.fori_loop(0, blocks, finish, 0)

    def unplace(at, carry):
        target = pl.ds(pl.multiple_of(at * half, half), half)
        source = pl.ds(pl.multiple_of(order_ref[at] * half, half), half)
        att_ref[target, :] = att_s[source, :]
        gmix_ref[target, :] = gm_s[source, :]
        return carry

    lax.fori_loop(0, halves, unplace, 0)


def attention_sorted(order, mixed, grad_att):
    count, width = grad_att.shape
    block = math.gcd(256, count)
    cosine, sine = tables(jnp.arange(count, dtype=jnp.int32), ROT)
    vmem = pl.BlockSpec(memory_space=pltpu.VMEM)
    pairs = count * count // 2 * (width // HEAD)
    return pl.pallas_call(
        functools.partial(attention_kernel, block),
        out_shape=(
            jax.ShapeDtypeStruct((count, width), BF),
            jax.ShapeDtypeStruct((count, 3 * width), BF),
        ),
        in_specs=[pl.BlockSpec(memory_space=pltpu.SMEM)] + [vmem] * 4,
        out_specs=(vmem, vmem),
        scratch_shapes=[
            pltpu.VMEM((count, 3 * width), F32),
            pltpu.VMEM((count, width), F32),
            pltpu.VMEM((count, HEAD), BF),
            pltpu.VMEM((count, HEAD), BF),
            pltpu.VMEM((count, HEAD), BF),
            pltpu.VMEM((HEAD, count), BF),
            pltpu.VMEM((HEAD, count), BF),
            pltpu.VMEM((count, HEAD), BF),
            pltpu.VMEM((HEAD, count), F32),
            pltpu.VMEM((count, block), F32),
            pltpu.VMEM((count, HEAD), F32),
            pltpu.VMEM((count, HEAD), F32),
            pltpu.VMEM((count, width), BF),
            pltpu.VMEM((count, 3 * width), BF),
        ],
        compiler_params=pltpu.CompilerParams(vmem_limit_bytes=40 * 1024 * 1024),
        cost_estimate=pl.CostEstimate(
            flops=12 * pairs * HEAD, bytes_accessed=count * width * 30, transcendentals=pairs
        ),
    )(order, mixed, grad_att, cosine, sine)


def attention_blocks(own_place, places, mixed, grad_att, gather, scatter):
    count, width = grad_att.shape
    heads = width // HEAD
    scale = 1.0 / math.sqrt(HEAD)
    cosine, sine = tables(own_place, ROT)
    cosine, sine = cosine[:, None, :], sine[:, None, :]
    kinds = [mixed[:, kind * width : (kind + 1) * width].reshape(count, heads, HEAD) for kind in range(3)]
    queries = turned(kinds[0], cosine, sine).astype(BF)
    keys = gather(turned(kinds[1], cosine, sine).astype(BF))
    values = gather(kinds[2].astype(BF))
    grad_att = grad_att.reshape(count, heads, HEAD)
    block = math.gcd(128, count)

    def one(at, carry):
        key_grad, value_grad, attended, query_grad = carry
        query = lax.dynamic_slice_in_dim(queries, at * block, block)
        grad = lax.dynamic_slice_in_dim(grad_att, at * block, block)
        place = lax.dynamic_slice_in_dim(own_place, at * block, block)
        visible = (place[:, None] >= places[None, :])[None]
        scores = jnp.einsum("qhe,khe->hqk", query, keys, preferred_element_type=F32) * scale
        scores = jnp.where(visible, scores, NEG)
        top = jnp.max(scores, axis=-1, keepdims=True)
        expo = jnp.where(visible, jnp.exp(scores - top), 0.0)
        total = jnp.sum(expo, axis=-1)
        summed = jnp.einsum("hqk,khe->qhe", expo.astype(BF), values, preferred_element_type=F32)
        attend = summed / jnp.transpose(total)[..., None]
        delta = jnp.transpose(jnp.sum(grad.astype(F32) * attend, axis=-1))
        prob = expo / total[..., None]
        dprob = jnp.einsum("qhe,khe->hqk", grad, values, preferred_element_type=F32)
        dscore = (prob * (dprob - delta[..., None])).astype(BF)
        part_q = jnp.einsum("hqk,khe->qhe", dscore, keys, preferred_element_type=F32) * scale
        key_grad += jnp.einsum("hqk,qhe->khe", dscore, query, preferred_element_type=F32) * scale
        value_grad += jnp.einsum("hqk,qhe->khe", prob.astype(BF), grad, preferred_element_type=F32)
        attended = lax.dynamic_update_slice_in_dim(attended, attend.astype(BF), at * block, 0)
        query_grad = lax.dynamic_update_slice_in_dim(query_grad, part_q, at * block, 0)
        return (key_grad, value_grad, attended, query_grad)

    zeros = jnp.zeros(keys.shape, F32)
    own = jnp.zeros((count, heads, HEAD), F32)
    key_grad, value_grad, attended, query_grad = lax.fori_loop(
        0, count // block, one, (zeros, zeros, own.astype(BF), own)
    )
    key_grad, value_grad = scatter(key_grad), scatter(value_grad)
    grad_mixed = jnp.concatenate(
        [
            turned(query_grad, cosine, -sine).astype(BF).reshape(count, width),
            turned(key_grad, cosine, -sine).astype(BF).reshape(count, width),
            value_grad.astype(BF).reshape(count, width),
        ],
        axis=1,
    )
    return attended.reshape(count, width), grad_mixed


def gelu_tanh(value):
    return jax.nn.gelu(value, approximate=True)


def local(
    tokens, block_order, ln_gain, ln_bias, qkv_weight, qkv_bias, out_weight, fc1_weight, fc1_bias,
    fc2_weight, out_bias, cotangent,
):
    devices = lax.axis_size("ctx")
    myself = lax.axis_index("ctx")
    rows_here, features = tokens.shape
    weight_rows = qkv_weight.shape[0]
    half = devices * rows_here // block_order.shape[0]
    heads_here = qkv_weight.shape[2] // HEAD
    columns = math.gcd(devices, heads_here)
    groups = devices // columns
    mine = myself % columns
    width = qkv_weight.shape[2] // columns
    hidden = fc1_weight.shape[1] // columns
    count = columns * rows_here
    side = [[r * columns + c for c in range(columns)] for r in range(groups)]
    across = [[r * columns + c for r in range(groups)] for c in range(columns)]

    def group_gather(value):
        return lax.all_gather(value, "ctx", axis=0, tiled=True, axis_index_groups=side)

    def group_scatter(value):
        return lax.psum_scatter(
            value, "ctx", scatter_dimension=0, tiled=True, axis_index_groups=side
        )

    packed = jnp.concatenate(
        [
            qkv_weight.reshape(weight_rows, 3, columns, width).transpose(2, 0, 1, 3).reshape(
                columns, weight_rows, 3 * width
            ),
            fc1_weight.reshape(weight_rows, columns, hidden).transpose(1, 0, 2),
            out_weight.reshape(weight_rows, columns, width).transpose(1, 0, 2),
            fc2_weight.reshape(weight_rows, columns, hidden).transpose(1, 0, 2),
        ],
        axis=2,
    )
    if groups > 1:
        packed = jnp.tile(packed, (groups, 1, 1))
    packed = lax.all_to_all(packed, "ctx", split_axis=0, concat_axis=0, tiled=True)
    packed = packed.reshape(devices * weight_rows, packed.shape[2])
    inner_width = 3 * width + hidden
    w_in, w_out = packed[:, :inner_width], packed[:, inner_width:]
    bias_in = jnp.concatenate(
        [
            lax.dynamic_slice_in_dim(qkv_bias, mine * width, width, 1).reshape(-1),
            lax.dynamic_slice_in_dim(fc1_bias, mine * hidden, hidden, 0),
        ]
    )

    x_all = group_gather(tokens)
    g_all = group_gather(cotangent)
    inputs = x_all.astype(F32)
    center = inputs - jnp.mean(inputs, axis=-1, keepdims=True)
    inv_std = lax.rsqrt(jnp.mean(center * center, axis=-1, keepdims=True) + EPS)
    unit = center * inv_std
    normed = (unit * ln_gain + ln_bias).astype(BF)

    mixed = mm(normed, w_in[:, : 3 * width]) + bias_in[: 3 * width]
    upward = mm(normed, w_in[:, 3 * width :]) + bias_in[3 * width :]
    activated, gelu_back = jax.vjp(gelu_tanh, upward)
    activated = activated.astype(BF)
    grad_att = mm(g_all, w_out[:, :width]).astype(BF)
    grad_up = gelu_back(mm(g_all, w_out[:, width:]))[0].astype(BF)
    if groups == 1:
        attended, grad_mixed = attention_sorted(block_order, mixed, grad_att)
    else:
        places = (block_order[:, None] * half + jnp.arange(half, dtype=jnp.int32)[None, :]).reshape(-1)
        attended, grad_mixed = attention_blocks(
            lax.dynamic_slice_in_dim(places, (myself // columns) * count, count),
            places,
            mixed,
            grad_att,
            lambda value: lax.all_gather(
                value, "ctx", axis=0, tiled=True, axis_index_groups=across
            ),
            lambda value: lax.psum_scatter(
                value, "ctx", scatter_dimension=0, tiled=True, axis_index_groups=across
            ),
        )
    hiddens = jnp.concatenate([attended, activated], axis=1)
    grads = jnp.concatenate([grad_mixed, grad_up], axis=1)

    branches = group_scatter(mm(hiddens, w_out, NT).astype(BF))
    normed_part = mm(grads, w_in, NT)
    branches, own_normed = lax.psum(
        (branches, group_scatter(normed_part.astype(BF))), "tp"
    )
    outer = mm(g_all, hiddens, TN).astype(BF)
    inner = mm(normed, grads, TN).astype(BF)
    back = jnp.concatenate([inner, outer], axis=1).reshape(devices, weight_rows, -1)
    back = lax.all_to_all(back, "ctx", split_axis=0, concat_axis=0, tiled=True)
    back = back.reshape(groups, columns, weight_rows, -1)
    back = back[0].astype(F32) if groups == 1 else jnp.sum(back.astype(F32), axis=0)

    def spread(piece, kinds):
        piece = piece.reshape(columns, weight_rows, kinds, -1).transpose(1, 2, 0, 3)
        return piece.reshape(weight_rows, kinds, -1)

    qkv_grad = spread(back[:, :, : 3 * width], 3)
    fc1_grad = spread(back[:, :, 3 * width : inner_width], 1)[:, 0]
    out_grad = spread(back[:, :, inner_width : inner_width + width], 1)[:, 0]
    fc2_grad = spread(back[:, :, inner_width + width :], 1)[:, 0]

    column_sums = jnp.sum(grads.astype(F32), axis=0)
    qkv_sums = lax.dynamic_update_slice(
        jnp.zeros(qkv_bias.shape, F32), column_sums[: 3 * width].reshape(3, width), (0, mine * width)
    )
    fc1_sums = lax.dynamic_update_slice(
        jnp.zeros(fc1_bias.shape, F32), column_sums[3 * width :], (mine * hidden,)
    )
    g_sum = jnp.sum(g_all.astype(F32), axis=0) / columns
    qkv_sums, fc1_sums, g_sum = lax.psum((qkv_sums, fc1_sums, g_sum), "ctx")
    gain_sum, shift_sum = lax.psum(
        (jnp.sum(unit * normed_part, axis=0), jnp.sum(normed_part, axis=0)), ("ctx", "tp")
    )

    own = tokens.astype(F32)
    center = own - jnp.mean(own, axis=-1, keepdims=True)
    inv_std = lax.rsqrt(jnp.mean(center * center, axis=-1, keepdims=True) + EPS)
    unit = center * inv_std
    output = own + branches.astype(F32) + out_bias
    grad_unit = own_normed.astype(F32) * ln_gain
    input_grad = cotangent.astype(F32) + inv_std * (
        grad_unit
        - jnp.mean(grad_unit, axis=-1, keepdims=True)
        - unit * jnp.mean(grad_unit * unit, axis=-1, keepdims=True)
    )
    return (
        output, input_grad, gain_sum, shift_sum, qkv_grad, qkv_sums, out_grad, fc1_grad, fc1_sums,
        fc2_grad, g_sum,
    )


def solution(mesh):
    rows, tall = P("ctx", None), P("ctx", "tp")
    kinds, bias = P("ctx", None, "tp"), P(None, "tp")
    return jax.shard_map(
        local,
        mesh=mesh,
        in_specs=(rows, P(), P(), P(), kinds, bias, tall, tall, P("tp"), tall, P(), rows),
        out_specs=(rows, rows, P(), P(), kinds, bias, tall, tall, P("tp"), tall, P()),
        check_vma=False,
    )
```

time: 1800 us -> 667 us (0.37)
  waiting for transfers between devices: 1400 us -> 289 us
  matrix products: 232 us -> 61.4 us
  blocking collectives: 61.9 us -> 179 us
  Pallas kernels: 0 us -> 41.8 us
    reduce_scatter x2, waiting for transfers between devices: 876 us -> 109 us  [group_scatter(): lax.psum_scatter(value, 'ctx', scatter_dimension=0, tiled=True, axis_inde...]
    ppermute x62 -> x0, waiting for transfers between devices: 291 us -> none  [passed_along(): return lax.ppermute(value, axis, pairs)]
    dot_general x92 -> x8, matrix products: 232 us -> 61.4 us  [mm(): return lax.dot_general(left, right, dims, preferred_element_type=F32)]
    all_gather x6 -> x2, waiting for transfers between devices: 224 us -> 82.6 us  [group_gather(): lax.all_gather(value, 'ctx', axis=0, tiled=True, axis_index_groups=side)]
    psum x1 -> x2, blocking collectives: 61.9 us -> 179 us  [the longest x1 118 us: local(): lax.psum((jnp.sum(unit * normed_part, axis=0), jnp.sum(normed_part, axis=...]
    all_to_all x0 -> x2, waiting for transfers between devices: none -> 95.6 us  [the longest x1 95.6 us: local(): lax.all_to_all(packed, 'ctx', split_axis=0, concat_axis=0, tiled=True)]
    pallas_call x0 -> x1, Pallas kernels: none -> 41.8 us  [attention_sorted(): pl.pallas_call(functools.partial(attention_kernel, block), out_shape=(jax...]
    ppermute x62 -> x0, starting transfers between devices: 21.3 us -> none  [passed_along(): return lax.ppermute(value, axis, pairs)]
  transfers between devices with their start and end apart: 71 -> 7, of which waited for: 66 -> 5; matrix products, arithmetic and copies ran while one was open for 15% -> 11% of each run, Pallas kernels for 0% -> 0%
where the time goes in v1:
time: 667 us; the launch traced here: 662 us
  waiting for transfers between devices  289 us (43%)
  blocking collectives  179 us (27%)
  matrix products  61.4 us (9%)
  Pallas kernels  41.8 us (6%)
  other arithmetic  34.5 us (5%)
  local copies, waits for them, and re-layouts  30.1 us (5%)
  between operations  14.4 us (2%)
  starting transfers between devices  11.7 us (2%)
    psum x1, blocking collectives, local(): lax.psum((jnp.sum(unit * normed_part, axis=0), jnp.sum(normed_part, axis=...  118 us
    reduce_scatter x2, waiting for transfers between devices, group_scatter(): lax.psum_scatter(value, 'ctx', scatter_dimension=0, tiled=True, axis_inde...  109 us
    all_to_all x1, waiting for transfers between devices, local(): lax.all_to_all(packed, 'ctx', split_axis=0, concat_axis=0, tiled=True)  95.6 us
    all_gather x2, waiting for transfers between devices, group_gather(): lax.all_gather(value, 'ctx', axis=0, tiled=True, axis_index_groups=side)  82.6 us
    dot_general x8, matrix products, mm(): return lax.dot_general(left, right, dims, preferred_element_type=F32)  61.4 us
    psum x1, blocking collectives, local(): qkv_sums, fc1_sums, g_sum = lax.psum((qkv_sums, fc1_sums, g_sum), 'ctx')  60.9 us
    pallas_call x1, Pallas kernels, attention_sorted(): pl.pallas_call(functools.partial(attention_kernel, block), out_shape=(jax...  41.8 us
    unnamed x48, local copies, waits for them, and re-layouts  17.3 us
  transfers between devices with their start and end apart: 7, of which 5 were waited for; matrix products, arithmetic and copies ran while one was open for 11% of the time, Pallas kernels for 0%

profile of v1, /device:TPU:0, one launch (start us, length us, event | category | flops | bytes accessed | tf_op | source)
XLA Modules:
  0.0 661.6 jit_solution(1317329616229965693)
XLA Ops:
  7.2 0.7 all-gather.3.cloned.1.call-update
  8.0 0.7 all-gather.5.cloned.1.call-update
  8.7 1.1 copy.65
  9.8 1.5 copy.62
  12.1 1.6 copy.66
  13.7 1.8 pad_maximum_fusion
  15.5 7.4 %all-to-all-start = ((bf16[16,128,768]{1,2,0:T(8,128)(2,1)}), bf16[16,128,768]{1,2,0:T(8,128)(2,1)}, u32[]{:S(2)}, u32[]{:S(2)}) async-start(bf16[16,128,768]{1,2,0:T(8,128)(2,1)} %pad_maximum_fusion), calls=%async_computation | async-start | bytes 6291456 | tf_op jit(solution)/shard_map/all_to_all | solution.py:296
  23.2 0.8 dynamic_slice.7
  24.0 3.7 multiply_sine_fusion
  27.6 95.6 %all-to-all-done = bf16[16,128,768]{1,2,0:T(8,128)(2,1)} async-done(((bf16[16,128,768]{1,2,0:T(8,128)(2,1)}), bf16[16,128,768]{1,2,0:T(8,128)(2,1)}, u32[]{:S(2)}, u32[]{:S(2)}) %all-to-all-start) | async-done | bytes 3145760 | tf_op jit(solution)/shard_map/all_to_all | solution.py:296
  123.2 4.8 copy.67
  128.0 9.9 %all-gather.3.cloned.1.call-done = bf16[2048,2048]{1,0:T(8,128)(2,1)} async-done(((bf16[128,2048]{1,0:T(8,128)(2,1)}), bf16[2048,2048]{1,0:T(8,128)(2,1)}) %all-gather.3.cloned.1.call-update) | async-done | bytes 8388624 | tf_op jit(solution)/shard_map/all_gather | solution.py:276
  137.9 4.7 convert_reduce_fusion
  142.6 1.1 copy-done.6
  143.6 2.3 fusion.7
  146.0 72.7 %all-gather.5.cloned.1.call-done = bf16[2048,2048]{1,0:T(8,128)(2,1)} async-done(((bf16[128,2048]{1,0:T(8,128)(2,1)}), bf16[2048,2048]{1,0:T(8,128)(2,1)}) %all-gather.5.cloned.1.call-update) | async-done | bytes 8388624 | tf_op jit(solution)/shard_map/all_gather | solution.py:276
  218.7 6.6 convolution_convert_fusion.3
  225.3 1.0 copy.70
  226.3 5.9 fusion.5
  232.3 4.6 convolution_add_fusion.1.mixed_ref
  236.9 41.8 %shard_map.203 = (bf16[2048,64]{1,0:T(8,128)(2,1)S(1)}, bf16[2048,192]{1,0:T(8,128)(2,1)S(1)}) custom-call(s32[32]{0:T(128)S(1)} %copy-done.5, f32[2048,192]{1,0:T(8,128)S(1)} %convolution_add_fusion.1.mixed_ref, bf16[2048,64]{1,0:T(8,128)(2,1)S(1)} %bitcast.51, f32[2048,16]{1,0:T(8,128)S(1)} %get-tuple-element.65.cos_ref, ...), custom_call_target="tpu_custom_call" | custom-call | flops 1610612736 | bytes 3932160 | tf_op jit(solution)/shard_map/pallas_call | solution.py:167
  278.7 0.8 copy-done.2
  279.5 0.7 copy.73
  280.2 8.0 %multiply_convert_fusion = (bf16[2048,256]{0,1:T(8,128)(2,1)}, f32[2048,256]{0,1:T(8,128)S(1)}) fusion(f32[256]{0:T(256)S(1)} %dynamic_slice.7, bf16[2048,2048]{1,0:T(8,128)(2,1)} %copy-done.8, bf16[2048,768]{1,0:T(8,128)(2,1)} %bitcast.60), kind=kOutput, calls=%fused_computation.34 | convolution fusion | flops 2152726528 | bytes 12583936 | tf_op jit(solution)/shard_map/dot_general | solution.py:23
  288.3 7.3 %fusion.15 = bf16[2048,256]{0,1:T(8,128)(2,1)S(1)} fusion(f32[2048,256]{0,1:T(8,128)S(1)} %get-tuple-element.67, bf16[2048,2048]{1,0:T(8,128)(2,1)} %all-gather.5.cloned.1.call-done, bf16[2048,768]{1,0:T(8,128)(2,1)S(1)} %bitcast.62), kind=kOutput, calls=%fused_computation.31 | convolution fusion | flops 2157969408 | bytes 12582912 | tf_op jit(solution)/shard_map/dot_general | solution.py:23
  295.6 9.5 %fusion.38 = (f32[2048]{0:T(1024)S(1)}, f32[2048]{0:T(1024)S(1)}, bf16[2048,2048]{1,0:T(8,128)(2,1)}) fusion(f32[2048]{0:T(1024)S(1)} %add_rsqrt_fusion, f32[2048]{0:T(1024)S(1)} %broadcast_multiply_fusion.1, bf16[2048,2048]{1,0:T(8,128)(2,1)S(1)} %bitcast.53, bf16[2048,768]{1,0:T(8,128)(2,1)S(1)} %bitcast.63, bf16[2048,256]{0,1:T(8,128)(2,1)S(1)} %fusion.15, ...), kind=kOutput, calls=%fused_computation.74 | convolution fusion | flops 3791122432 | bytes 20742144 | tf_op jit(solution)/shard_map/dot_general | solution.py:23
  306.4 10.3 %convolution_convert_fusion = bf16[2048,2048]{1,0:T(8,128)(2,1)} fusion(bf16[2048,768]{1,0:T(8,128)(2,1)} %bitcast.61, bf16[2048,256]{0,1:T(8,128)(2,1)} %get-tuple-element.66, bf16[2048,64]{0,1:T(8,128)(2,1)S(1)} %copy.72), kind=kOutput, calls=%fused_computation.11 | convolution fusion | flops 2691170304 | bytes 11272192 | tf_op jit(solution)/shard_map/dot_general | solution.py:23
  316.6 7.5 %fusion.8 = bf16[2048,320]{0,1:T(8,128)(2,1)S(1)} fusion(bf16[2048,2048]{1,0:T(8,128)(2,1)} %all-gather.5.cloned.1.call-done, bf16[2048,256]{0,1:T(8,128)(2,1)} %get-tuple-element.66, bf16[2048,64]{0,1:T(8,128)(2,1)S(1)} %copy.72), kind=kOutput, calls=%fused_computation.23 | convolution fusion | flops 2687631360 | bytes 11010048 | tf_op jit(solution)/shard_map/dot_general | solution.py:23
  324.1 7.7 %convolution_convert_fusion.1 = bf16[2048,448]{0,1:T(8,128)(2,1)S(1)} fusion(bf16[2048,2048]{1,0:T(8,128)(2,1)} %copy-done.8, bf16[2048,256]{0,1:T(8,128)(2,1)S(1)} %fusion.15, bf16[2048,192]{0,1:T(8,128)(2,1)S(1)} %copy.73), kind=kOutput, calls=%fused_computation.18 | convolution fusion | flops 3762683904 | bytes 12058624 | tf_op jit(solution)/shard_map/dot_general | solution.py:23
  331.8 2.5 copy_bitcast_fusion
  334.2 3.7 all-to-all-start.1
  338.0 1.2 convert_reduce_fusion.3
  339.3 1.3 fusion.27
  340.6 1.8 convert_reduce_fusion.2
  342.6 117.7 %all-reduce = (f32[2048]{0:T(1024)}, f32[2048]{0:T(1024)}) all-reduce(f32[2048]{0:T(1024)S(1)} %get-tuple-element.49, f32[2048]{0:T(1024)S(1)} %get-tuple-element.48), channel_id=1, replica_groups=mesh['ctx'=16,'tp'=2] {'ctx','tp'}, use_global_device_ids=true, to_apply=%region_11.12 | all-reduce | flops 4096 | bytes 32768 | tf_op jit(solution)/shard_map/psum | solution.py:370
  460.5 1.1 reduce-scatter.5.cloned.1.call-done
  461.6 108.3 %reduce-scatter.3.cloned.1.call-done = bf16[128,2048]{1,0:T(8,128)(2,1)} async-done(((bf16[2048,2048]{1,0:T(8,128)(2,1)}), bf16[128,2048]{1,0:T(8,128)(2,1)}) %reduce-scatter.3.cloned.1.call-update) | async-done | bytes 524304 | tf_op jit(solution)/shard_map/reduce_scatter | solution.py:279
  569.9 4.7 convert_reduce_fusion.1
  574.7 60.9 %all-reduce.1 = (f32[3,1024]{1,0:T(4,128)}, f32[4096]{0:T(1024)}, f32[2048]{0:T(1024)}) all-reduce(f32[3,1024]{1,0:T(4,128)S(1)} %dynamic_update_slice.6, f32[4096]{0:T(1024)S(1)} %slice_dynamic-update-slice_fusion, f32[2048]{0:T(1024)S(1)} %broadcast_multiply_fusion), channel_id=1, replica_groups=mesh['ctx'=16,'tp'=2] {'ctx'}, use_global_device_ids=true, to_apply=%region_15.16 | all-reduce | flops 9216 | bytes 73728 | tf_op jit(solution)/shard_map/psum | solution.py:369
  635.6 0.8 slice.67
  636.5 2.0 copy.77
  638.6 1.2 copy.75
  639.9 3.0 copy.76
  642.9 2.5 fusion.39
  645.4 3.0 copy.79
  648.5 1.8 copy.78
  650.3 1.4 fusion.32
  651.7 3.1 fusion.26
  (69 shorter events, 2.9 us)
Async XLA Ops:
  7.2 15.8 %copy-start = (f32[3,1024]{1,0:T(4,128)S(1)}, f32[3,1024]{1,0:T(4,128)}, u32[]{:S(2)}) copy-start(f32[3,1024]{1,0:T(4,128)} %param.17) | copy-start | bytes 36868
  7.2 4.2 copy-start.13
  7.2 130.7 %all-gather.3.cloned.1.call-start = ((), (), s32[]{:S(2)}) async-start(), calls=%async_computation.4 | async-start | bytes 8912896 | tf_op jit(solution)/shard_map/all_gather | solution.py:276
  7.9 210.8 %all-gather.5.cloned.1.call-start = ((), (), s32[]{:S(2)}) async-start(), calls=%async_computation.5 | async-start | bytes 8912896 | tf_op jit(solution)/shard_map/all_gather | solution.py:276
  15.5 107.7 %all-to-all-start = ((bf16[16,128,768]{1,2,0:T(8,128)(2,1)}), bf16[16,128,768]{1,2,0:T(8,128)(2,1)}, u32[]{:S(2)}, u32[]{:S(2)}) async-start(bf16[16,128,768]{1,2,0:T(8,128)(2,1)} %pad_maximum_fusion), calls=%async_computation | async-start | bytes 6291456 | tf_op jit(solution)/shard_map/all_to_all | solution.py:296
  22.9 438.7 %reduce-scatter.5.cloned.1.call-start = ((), (), s32[]{:S(2)}) async-start(), calls=%async_computation.7 | async-start | bytes 8912896 | tf_op jit(solution)/shard_map/reduce_scatter | solution.py:279
  137.9 5.8 copy-start.6
  218.7 7.6 %copy-start.15 = (f32[2048]{0:T(1024)S(1)}, f32[2048]{0:T(1024)}, u32[]{:S(2)}) copy-start(f32[2048]{0:T(1024)} %param.14) | copy-start | bytes 24580
  218.7 7.6 %copy-start.16 = (f32[2048]{0:T(1024)S(1)}, f32[2048]{0:T(1024)}, u32[]{:S(2)}) copy-start(f32[2048]{0:T(1024)} %param.15) | copy-start | bytes 24580
  232.2 4.7 copy-start.8
  232.2 4.7 copy-start.4
  232.3 4.7 copy-start.5
  278.7 0.8 copy-start.2
  280.2 43.9 %copy-start.11 = (bf16[2048,192]{0,1:T(8,128)(2,1)}, bf16[2048,192]{0,1:T(8,128)(2,1)S(1)}, u32[]{:S(2)}) copy-start(bf16[2048,192]{0,1:T(8,128)(2,1)S(1)} %copy.73) | copy-start | bytes 2359300
  280.2 8.0 %copy-start.10 = (bf16[16,128,768]{2,1,0:T(8,128)(2,1)S(1)}, bf16[16,128,768]{2,1,0:T(8,128)(2,1)}, u32[]{:S(2)}) copy-start(bf16[16,128,768]{2,1,0:T(8,128)(2,1)} %copy.67) | copy-start | bytes 9437188
  280.2 15.3 %slice-start = ((s8[8388608]{0:T(1024)(128)(4,1)}), s8[4194304]{0:T(1024)(128)(4,1)S(1)}, s32[]{:S(2)}) async-start(s8[8388608]{0:T(1024)(128)(4,1)} %bitcast.52), calls=%async_computation.9 | async-start | bytes 8388608
  288.3 7.3 %slice-start.1 = ((s8[8388608]{0:T(1024)(128)(4,1)}), s8[4194304]{0:T(1024)(128)(4,1)S(1)}, s32[]{:S(2)}) async-start(s8[8388608]{0:T(1024)(128)(4,1)} %bitcast.52), calls=%async_computation.10 | async-start | bytes 8388608
  295.6 28.5 %copy-start.14 = (bf16[2048,256]{0,1:T(8,128)(2,1)}, bf16[2048,256]{0,1:T(8,128)(2,1)S(1)}, u32[]{:S(2)}) copy-start(bf16[2048,256]{0,1:T(8,128)(2,1)S(1)} %fusion.15) | copy-start | bytes 3145732
  305.1 1.0 copy-start.3
  305.1 264.8 %reduce-scatter.3.cloned.1.call-start = ((), (), s32[]{:S(2)}) async-start(), calls=%async_computation.6 | async-start | bytes 8912896 | tf_op jit(solution)/shard_map/reduce_scatter | solution.py:279
  334.2 301.4 %all-to-all-start.1 = ((bf16[16,128,768]{1,2,0:T(8,128)(2,1)}), bf16[16,128,768]{1,2,0:T(8,128)(2,1)S(1)}, u32[]{:S(2)}, u32[]{:S(2)}) async-start(bf16[16,128,768]{1,2,0:T(8,128)(2,1)} %copy_bitcast_fusion), calls=%async_computation.3 | async-start | bytes 6291456 | tf_op jit(solution)/shard_map/all_to_all | solution.py:348
  338.0 312.3 %all-reduce.5.cloned.1.call-start = ((), (), s32[]{:S(2)}) async-start(), calls=%async_computation.8 | async-start | bytes 2097152 | tf_op jit(solution)/shard_map/psum | solution.py:342
  645.4 3.0 copy-start.9
  648.5 1.8 copy-start.7
  648.5 3.3 copy-start.12
  648.5 3.3 copy-start.17
  648.5 6.4 copy-start.1
Sparse Core Ops, SparseCore 0:
  10.2 127.6 all-gather.2
  140.0 78.6 all-gather.4
  305.3 156.2 reduce-scatter.4
  465.5 104.3 reduce-scatter.2
  572.1 39.9 all-reduce.4
